TPU v7x, 128 devices: a whole 4x4x4 slice. The times are simulated.
128 devices in a mesh: blk: 8 (over z, y_hi), tok: 16 (over x, y_lo, core).
Axes of the slice: x: 4, y: 4 (y_hi: 2, y_lo: 2; y = y_hi * 2 + y_lo), z: 4, core: 2. Of those that a mesh axis runs over, the one named last changes fastest.
Arguments:
- inputs: float32 [4096, 16384], P('tok', 'blk'), may hold values from -6 to 6
- first_factor: float32 [16, 1024, 1024], P('blk', 'tok'), may hold values from -0.1875 to 0.1875
- second_factor: float32 [16, 1024, 1024], P('blk', 'tok'), may hold values from -0.1875 to 0.1875
- cotangent: float32 [4096, 16384], P('tok', 'blk'), may hold values from -6 to 6
Outputs:
- input_grad: float32 [4096, 16384], P('tok', 'blk')
- first_grad: float32 [16, 1024, 1024], P('blk', 'tok')
- second_grad: float32 [16, 1024, 1024], P('blk', 'tok')
All inputs are finite; a program needn't handle non-finite values.
Results may differ from a plain program's by a relative error of at most 0.00013.
Values sent between devices are 32-bit elements; how exact they have to be, the bound alone decides.
A program may use at most 128 MiB of HBM per device.

v0:
```python
import math
import jax
import jax.numpy as jnp
from jax import lax
from jax.sharding import PartitionSpec as P


def body(inputs, first_factor, second_factor, cotangent):
    hp = lax.Precision.HIGHEST
    local_blocks = first_factor.shape[0]
    order = first_factor.shape[2]
    blocks = local_blocks * lax.axis_size("blk")
    group = order // blocks
    count = inputs.shape[0]
    xb = inputs.reshape(count, local_blocks, order)
    first_whole, second_whole = (
        lax.all_gather(first_factor, "tok", axis=1, tiled=True),
        lax.all_gather(second_factor, "tok", axis=1, tiled=True),
    )
    first_view = first_whole.reshape(local_blocks, order, blocks, group)
    first = jnp.einsum("tbi,bisg->stbg", xb, first_view, precision=hp).reshape(
        blocks, count, local_blocks * group
    )
    mixed = lax.all_to_all(first, "blk", split_axis=0, concat_axis=2, tiled=True)
    second = jnp.einsum("btk,bko->tbo", mixed, second_whole, precision=hp)
    normal_cdf = 0.5 * (1.0 + jax.scipy.special.erf(second / math.sqrt(2.0)))
    density = jnp.exp(-0.5 * second * second) / math.sqrt(2.0 * math.pi)
    delta_second = cotangent.reshape(count, local_blocks, order) * (normal_cdf + second * density)
    second_grad = jnp.einsum("btk,tbo->bko", mixed, delta_second, precision=hp)
    delta_mixed = jnp.einsum("tbo,bko->btk", delta_second, second_whole, precision=hp)
    delta_first = lax.all_to_all(delta_mixed, "blk", split_axis=2, concat_axis=0, tiled=True)
    delta_view = delta_first.reshape(blocks, count, local_blocks, group)
    first_grad = jnp.einsum("tbi,stbg->bisg", xb, delta_view, precision=hp).reshape(
        local_blocks, order, order
    )
    input_grad = jnp.einsum("stbg,bisg->tbi", delta_view, first_view, precision=hp).reshape(
        count, local_blocks * order
    )
    first_out, second_out = (
        lax.psum_scatter(first_grad, "tok", scatter_dimension=1, tiled=True),
        lax.psum_scatter(second_grad, "tok", scatter_dimension=1, tiled=True),
    )
    return (input_grad, first_out, second_out)


def solution(mesh):
    placed = (P("tok", "blk"), P("blk", "tok", None), P("blk", "tok", None), P("tok", "blk"))
    return jax.shard_map(
        body,
        mesh=mesh,
        in_specs=placed,
        out_specs=(P("tok", "blk"), P("blk", "tok", None), P("blk", "tok", None)),
        check_vma=False,
    )
```

profile of v0, /device:TPU:5, one launch (start us, length us, event | category | flops | bytes accessed | tf_op | source)
XLA Modules:
  0.0 389.0 jit_solution(9547876401872659460)
XLA Ops:
  7.2 0.0 all-gather.3.cloned.1.call-start
  7.2 0.7 all-gather.3.cloned.1.call-update
  7.9 0.0 all-gather.5.cloned.1.call-start
  7.9 0.7 all-gather.5.cloned.1.call-update
  8.6 3.0 reshape.30
  11.7 0.0 copy-start.2
  11.7 52.4 %all-gather.3.cloned.1.call-done = f32[2,1024,1024]{2,1,0:T(8,128)} async-done(((f32[2,64,1024]{2,1,0:T(8,128)}), f32[2,1024,1024]{2,1,0:T(8,128)}) %all-gather.3.cloned.1.call-update) | async-done | bytes 8388624 | tf_op jit(solution)/shard_map/all_gather | solution.py:17
  64.1 8.7 %copy.43 = f32[2,1024,1024]{1,2,0:T(8,128)} copy(f32[2,1024,1024]{2,1,0:T(8,128)} %all-gather.3.cloned.1.call-done) | data formatting | bytes 16777216 | tf_op jit(solution)/shard_map/all_gather | solution.py:17
  72.9 0.0 copy-done.2
  72.9 9.1 %fusion.15 = f32[16,256,2,64]{1,3,0,2:T(8,128)S(1)} fusion(f32[2,1024,16,64]{1,3,2,0:T(8,128)} %bitcast.43, f32[256,2,1024,1]{2,1,0,3:T(2,128)S(1)} %bitcast.46), kind=kOutput, calls=%fused_computation.17 | convolution fusion | flops 6442450944 | bytes 12582912 | tf_op jit(solution)/shard_map/tbi,bisg->stbg/dot_general | solution.py:21
  82.0 1.5 copy.45
  83.6 6.6 %all-to-all-start = ((f32[16,256,128]{1,2,0:T(8,128)}), f32[16,256,128]{1,2,0:T(8,128)S(1)}, u32[]{:S(2)}, u32[]{:S(2)}) async-start(f32[16,256,128]{1,2,0:T(8,128)} %bitcast.49), calls=%async_computation | async-start | bytes 4194304 | tf_op jit(solution)/shard_map/all_to_all | solution.py:24
  90.2 0.2 reduce-scatter.5.cloned.1.call-start
  90.4 2.9 copy.42
  93.3 2.9 copy.48
  96.3 21.9 %all-to-all-done = f32[16,256,128]{1,2,0:T(8,128)S(1)} async-done(((f32[16,256,128]{1,2,0:T(8,128)}), f32[16,256,128]{1,2,0:T(8,128)S(1)}, u32[]{:S(2)}, u32[]{:S(2)}) %all-to-all-start) | async-done | bytes 2097184 | tf_op jit(solution)/shard_map/all_to_all | solution.py:24
  118.2 1.8 copy.47
  120.0 1.7 all_to_all.27
  121.7 15.9 %all-gather.5.cloned.1.call-done = f32[2,1024,1024]{2,1,0:T(8,128)} async-done(((f32[2,64,1024]{2,1,0:T(8,128)}), f32[2,1024,1024]{2,1,0:T(8,128)}) %all-gather.5.cloned.1.call-update) | async-done | bytes 8388624 | tf_op jit(solution)/shard_map/all_gather | solution.py:18
  137.6 10.3 %fusion.6 = f32[256,2,1024]{2,0,1:T(8,128)S(1)} fusion(f32[256,2,1024]{2,0,1:T(8,128)} %copy.48, f32[2,256,1024]{2,1,0:T(8,128)S(1)} %all_to_all.27, f32[2,1024,1024]{2,1,0:T(8,128)} %all-gather.5.cloned.1.call-done), kind=kOutput, calls=%fused_computation.7 | convolution fusion | flops 6447169536 | bytes 14680064 | tf_op jit(solution)/shard_map/btk,bko->tbo/dot_general | solution.py:25
  147.8 0.0 copy-start
  147.8 1.3 copy-done
  149.2 9.0 %fusion.22 = f32[2,1024,1024]{2,1,0:T(8,128)} fusion(f32[2,256,1024]{2,1,0:T(8,128)S(1)} %all_to_all.27, f32[256,2,1024]{2,0,1:T(8,128)S(1)} %fusion.6), kind=kOutput, calls=%fused_computation.20 | convolution fusion | flops 6442450944 | bytes 12582912 | tf_op jit(solution)/shard_map/btk,tbo->bko/dot_general | solution.py:29
  158.1 0.0 copy-start.1
  158.1 0.0 reduce-scatter.5.cloned.1.call-update
  158.1 0.0 reduce-scatter.3.cloned.1.call-start
  158.2 1.5 copy-done.1
  159.7 10.6 %fusion.21 = f32[2,256,1024]{2,1,0:T(8,128)} fusion(f32[256,2,1024]{2,0,1:T(8,128)S(1)} %copy-done.1, f32[2,1024,1024]{2,1,0:T(8,128)} %all-gather.5.cloned.1.call-done), kind=kOutput, calls=%fused_computation.19 | convolution fusion | flops 6442450944 | bytes 12582912 | tf_op jit(solution)/shard_map/tbo,bko->btk/dot_general | solution.py:30
  170.3 2.9 copy.49
  173.1 58.0 %all_to_all.33 = f32[2,256,1024]{1,0,2:T(2,128)S(1)} all-to-all(f32[2,256,1024]{1,0,2:T(2,128)S(1)} %copy.49), channel_id=1, replica_groups=mesh['blk'=8,'tok'=16] {'blk'}, dimensions={2} | all-to-all | bytes 4194304 | tf_op jit(solution)/shard_map/all_to_all | solution.py:31
  231.2 0.2 copy.50
  231.3 0.0 copy-start.3
  231.4 0.1 copy.51
  231.5 1.5 copy-done.3
  233.0 9.2 %fusion.10 = f32[2,16,64,1024]{3,2,1,0:T(8,128)} fusion(f32[16,256,2,64]{1,3,2,0:T(8,128)S(1)} %bitcast.53, f32[256,2,1024,1]{2,1,0,3:T(2,128)S(1)} %bitcast.47), kind=kOutput, calls=%fused_computation.12 | convolution fusion | flops 6442450944 | bytes 12582912 | tf_op jit(solution)/shard_map/tbi,stbg->bisg/dot_general | solution.py:33
  242.2 8.7 %copy.56 = f32[2,1024,1024]{2,1,0:T(8,128)} copy(f32[2,1024,1024]{1,2,0:T(8,128)} %bitcast.45) | data formatting | bytes 16777216 | tf_op jit(solution)/shard_map/reshape | solution.py:33
  250.9 0.0 reduce-scatter.3.cloned.1.call-update
  250.9 10.5 %fusion.18 = f32[256,2,1024]{2,0,1:T(8,128)} fusion(f32[16,256,2,64]{1,3,2,0:T(8,128)S(1)} %bitcast.54, f32[2,1024,16,64]{1,3,2,0:T(8,128)} %bitcast.44), kind=kOutput, calls=%fused_computation.18 | convolution fusion | flops 6442450944 | bytes 12582912 | tf_op jit(solution)/shard_map/stbg,bisg->tbi/dot_general | solution.py:36
  261.4 1.9 copy.53
  263.3 1.8 copy.58
  265.1 15.8 %reduce-scatter.5.cloned.1.call-done = f32[2,64,1024]{2,1,0:T(8,128)} async-done(((f32[2,1024,1024]{2,1,0:T(8,128)}), f32[2,64,1024]{2,1,0:T(8,128)}) %reduce-scatter.5.cloned.1.call-update) | async-done | bytes 524304 | tf_op jit(solution)/shard_map/reduce_scatter | solution.py:41
  280.9 101.6 %reduce-scatter.3.cloned.1.call-done = f32[2,64,1024]{2,1,0:T(8,128)} async-done(((f32[2,1024,1024]{2,1,0:T(8,128)}), f32[2,64,1024]{2,1,0:T(8,128)}) %reduce-scatter.3.cloned.1.call-update) | async-done | bytes 524304 | tf_op jit(solution)/shard_map/reduce_scatter | solution.py:40
Async XLA Ops:
  7.2 57.0 %all-gather.3.cloned.1.call-start = ((), (), s32[]{:S(2)}) async-start(), calls=%async_computation.4 | async-start | bytes 8912896 | tf_op jit(solution)/shard_map/all_gather | solution.py:17
  7.9 129.7 %all-gather.5.cloned.1.call-start = ((), (), s32[]{:S(2)}) async-start(), calls=%async_computation.5 | async-start | bytes 8912896 | tf_op jit(solution)/shard_map/all_gather | solution.py:18
  11.7 61.2 %copy-start.2 = (f32[256,2,1024]{2,1,0:T(2,128)}, f32[256,2,1024]{2,1,0:T(2,128)S(1)}, u32[]{:S(2)}) copy-start(f32[256,2,1024]{2,1,0:T(2,128)S(1)} %reshape.30) | copy-start | bytes 6291460
  83.6 34.6 %all-to-all-start = ((f32[16,256,128]{1,2,0:T(8,128)}), f32[16,256,128]{1,2,0:T(8,128)S(1)}, u32[]{:S(2)}, u32[]{:S(2)}) async-start(f32[16,256,128]{1,2,0:T(8,128)} %bitcast.49), calls=%async_computation | async-start | bytes 4194304 | tf_op jit(solution)/shard_map/all_to_all | solution.py:24
  90.2 190.8 %reduce-scatter.5.cloned.1.call-start = ((), (), s32[]{:S(2)}) async-start(), calls=%async_computation.7 | async-start | bytes 8912896 | tf_op jit(solution)/shard_map/reduce_scatter | solution.py:41
  147.8 1.3 copy-start
  158.1 1.6 copy-start.1
  158.1 224.4 %reduce-scatter.3.cloned.1.call-start = ((), (), s32[]{:S(2)}) async-start(), calls=%async_computation.6 | async-start | bytes 8912896 | tf_op jit(solution)/shard_map/reduce_scatter | solution.py:40
  231.3 1.6 copy-start.3
Sparse Core Ops, SparseCore 0:
  9.7 54.4 all-gather.2
  65.8 71.7 all-gather.4
  158.3 122.6 reduce-scatter.4
  283.7 98.7 reduce-scatter.2
where the time goes:
time: 390 us; the launch traced here: 389 us
  waiting for transfers between devices  209 us (54%)
  matrix products  58.6 us (15%)
  blocking collectives  58 us (15%)
  local copies, waits for them, and re-layouts  42.6 us (11%)
  between operations  13.9 us (4%)
  starting transfers between devices  6.94 us (2%)
    reduce_scatter x1, waiting for transfers between devices, body(): lax.psum_scatter(first_grad, 'tok', scatter_dimension=1, tiled=True)  102 us
    all_to_all x1, blocking collectives, body(): lax.all_to_all(delta_mixed, 'blk', split_axis=2, concat_axis=0, tiled=True)  58 us
    all_gather x1, waiting for transfers between devices, body(): lax.all_gather(first_factor, 'tok', axis=1, tiled=True)  52.4 us
    all_to_all x1, waiting for transfers between devices, body(): lax.all_to_all(first, 'blk', split_axis=0, concat_axis=2, tiled=True)  21.9 us
    all_gather x1, waiting for transfers between devices, body(): lax.all_gather(second_factor, 'tok', axis=1, tiled=True)  15.9 us
    reduce_scatter x1, waiting for transfers between devices, body(): lax.psum_scatter(second_grad, 'tok', scatter_dimension=1, tiled=True)  15.8 us
    dot_general x1, matrix products, body(): jnp.einsum('tbo,bko->btk', delta_second, second_whole, precision=hp)  10.6 us
    dot_general x1, matrix products, body(): jnp.einsum('stbg,bisg->tbi', delta_view, first_view, precision=hp)  10.5 us
  transfers between devices with their start and end apart: 5, of which 5 were waited for; matrix products, arithmetic and copies ran while one was open for 20% of the time, Pallas kernels for 0%

commit v1 on v0

--- a/solution.py
+++ b/solution.py
@@ -3,6 +3,11 @@
 import jax.numpy as jnp
 from jax import lax
 from jax.sharding import PartitionSpec as P
+
+
+def gather_over(block, name, dim):
+    repeated = jnp.stack([block] * lax.axis_size(name))
+    return jnp.concatenate(lax.all_to_all(repeated, name, 0, 0), axis=dim)
 
 
 def body(inputs, first_factor, second_factor, cotangent):
@@ -15,7 +20,7 @@
     xb = inputs.reshape(count, local_blocks, order)
     first_whole, second_whole = (
         lax.all_gather(first_factor, "tok", axis=1, tiled=True),
-        lax.all_gather(second_factor, "tok", axis=1, tiled=True),
+        gather_over(second_factor, "tok", 1),
     )
     first_view = first_whole.reshape(local_blocks, order, blocks, group)
     first = jnp.einsum("tbi,bisg->stbg", xb, first_view, precision=hp).reshape(

time: 390 us -> 477 us (1.22)
  waiting for transfers between devices: 209 us -> 277 us
  local copies, waits for them, and re-layouts: 42.6 us -> 56.1 us
    all_gather x1, waiting for transfers between devices: 52.4 us -> 140 us  [body(): lax.all_gather(first_factor, 'tok', axis=1, tiled=True)]
    all_gather x1 -> x0, waiting for transfers between devices: 15.9 us -> none  [body(): lax.all_gather(second_factor, 'tok', axis=1, tiled=True)]
    reshape x0 -> x1, local copies, waits for them, and re-layouts: none -> 8.26 us  [gather_over(): return jnp.concatenate(lax.all_to_all(repeated, name, 0, 0), axis=dim)]
    all_to_all x1, waiting for transfers between devices: 21.9 us -> 13.7 us  [body(): lax.all_to_all(first, 'blk', split_axis=0, concat_axis=2, tiled=True)]
    all_to_all x0 -> x1, starting transfers between devices: none -> 6.15 us  [gather_over(): return jnp.concatenate(lax.all_to_all(repeated, name, 0, 0), axis=dim)]
    reduce_scatter x1, waiting for transfers between devices: 15.8 us -> 21.4 us  [body(): lax.psum_scatter(second_grad, 'tok', scatter_dimension=1, tiled=True)]
    another operation x0 -> x1, local copies, waits for them, and re-layouts: none -> 5.32 us  [gather_over(): repeated = jnp.stack([block] * lax.axis_size(name))]
  transfers between devices with their start and end apart: 5 -> 5, of which waited for: 5 -> 4; matrix products, arithmetic and copies ran while one was open for 20% -> 18% of each run, Pallas kernels for 0% -> 0%
where the time goes in v1:
time: 477 us; the launch traced here: 476 us
  waiting for transfers between devices  277 us (58%)
  matrix products  58.6 us (12%)
  blocking collectives  58.5 us (12%)
  local copies, waits for them, and re-layouts  56.1 us (12%)
  between operations  13.8 us (3%)
  starting transfers between devices  11.4 us (2%)
    all_gather x1, waiting for transfers between devices, body(): lax.all_gather(first_factor, 'tok', axis=1, tiled=True)  140 us
    reduce_scatter x1, waiting for transfers between devices, body(): lax.psum_scatter(first_grad, 'tok', scatter_dimension=1, tiled=True)  101 us
    all_to_all x1, blocking collectives, body(): lax.all_to_all(delta_mixed, 'blk', split_axis=2, concat_axis=0, tiled=True)  58.5 us
    reduce_scatter x1, waiting for transfers between devices, body(): lax.psum_scatter(second_grad, 'tok', scatter_dimension=1, tiled=True)  21.4 us
    all_to_all x1, waiting for transfers between devices, body(): lax.all_to_all(first, 'blk', split_axis=0, concat_axis=2, tiled=True)  13.7 us
    dot_general x1, matrix products, body(): jnp.einsum('tbo,bko->btk', delta_second, second_whole, precision=hp)  10.6 us
    dot_general x1, matrix products, body(): jnp.einsum('stbg,bisg->tbi', delta_view, first_view, precision=hp)  10.5 us
    dot_general x1, matrix products, body(): second = jnp.einsum('btk,bko->tbo', mixed, second_whole, precision=hp)  10.3 us
  transfers between devices with their start and end apart: 5, of which 4 were waited for; matrix products, arithmetic and copies ran while one was open for 18% of the time, Pallas kernels for 0%

profile of v1, /device:TPU:5, one launch (start us, length us, event | category | flops | bytes accessed | tf_op | source)
XLA Modules:
  0.0 475.9 jit_solution(2600200399602610627)
XLA Ops:
  7.2 0.0 all-gather.2.cloned.1.call-start
  7.2 0.7 all-gather.2.cloned.1.call-update
  7.9 5.3 %stack.2 = f32[16,2,64,1024]{3,2,1,0:T(8,128)} broadcast(f32[2,64,1024]{2,1,0:T(8,128)} %param.6), dimensions={1,2,3} | broadcast | bytes 8912896 | tf_op jit(solution)/shard_map/stack | solution.py:9
  13.2 6.1 %all-to-all-start.1 = ((f32[16,2,64,1024]{3,2,1,0:T(8,128)}), f32[16,2,64,1024]{3,2,1,0:T(8,128)}, u32[]{:S(2)}, u32[]{:S(2)}) async-start(f32[16,2,64,1024]{3,2,1,0:T(8,128)} %stack.2), calls=%async_computation.1 | async-start | bytes 16777216 | tf_op jit(solution)/shard_map/all_to_all | solution.py:10
  19.4 3.0 reshape.38
  22.4 0.0 copy-start.2
  22.4 140.2 %all-gather.2.cloned.1.call-done = f32[2,1024,1024]{2,1,0:T(8,128)} async-done(((f32[2,64,1024]{2,1,0:T(8,128)}), f32[2,1024,1024]{2,1,0:T(8,128)}) %all-gather.2.cloned.1.call-update) | async-done | bytes 8388624 | tf_op jit(solution)/shard_map/all_gather | solution.py:22
  162.7 8.7 %copy.44 = f32[2,1024,1024]{1,2,0:T(8,128)} copy(f32[2,1024,1024]{2,1,0:T(8,128)} %all-gather.2.cloned.1.call-done) | data formatting | bytes 16777216 | tf_op jit(solution)/shard_map/all_gather | solution.py:22
  171.4 0.0 copy-done.2
  171.4 9.2 %fusion.15 = f32[16,256,2,64]{1,3,0,2:T(8,128)S(1)} fusion(f32[2,1024,16,64]{1,3,2,0:T(8,128)} %bitcast.47, f32[256,2,1024,1]{2,1,0,3:T(2,128)S(1)} %bitcast.50), kind=kOutput, calls=%fused_computation.17 | convolution fusion | flops 6442450944 | bytes 12582912 | tf_op jit(solution)/shard_map/tbi,bisg->stbg/dot_general | solution.py:26
  180.6 1.6 copy.46
  182.1 0.0 all-to-all-done.1
  182.2 4.8 %all-to-all-start = ((f32[16,256,128]{1,2,0:T(8,128)}), f32[16,256,128]{1,2,0:T(8,128)S(1)}, u32[]{:S(2)}, u32[]{:S(2)}) async-start(f32[16,256,128]{1,2,0:T(8,128)} %bitcast.4), calls=%async_computation | async-start | bytes 4194304 | tf_op jit(solution)/shard_map/all_to_all | solution.py:29
  186.9 0.2 reduce-scatter.5.cloned.1.call-start
  187.1 2.9 copy.43
  190.0 2.9 copy.50
  192.9 8.3 %copy.49 = f32[2,16,64,1024]{3,2,1,0:T(8,128)} copy(f32[2,16,64,1024]{3,2,0,1:T(8,128)} %bitcast.8) | data formatting | bytes 16777216 | tf_op jit(solution)/shard_map/reshape | solution.py:10
  201.2 13.7 %all-to-all-done = f32[16,256,128]{1,2,0:T(8,128)S(1)} async-done(((f32[16,256,128]{1,2,0:T(8,128)}), f32[16,256,128]{1,2,0:T(8,128)S(1)}, u32[]{:S(2)}, u32[]{:S(2)}) %all-to-all-start) | async-done | bytes 2097184 | tf_op jit(solution)/shard_map/all_to_all | solution.py:29
  214.9 1.8 copy.48
  216.7 1.7 all_to_all.30
  218.4 10.3 %fusion.6 = f32[256,2,1024]{2,0,1:T(8,128)S(1)} fusion(f32[256,2,1024]{2,0,1:T(8,128)} %copy.50, f32[2,256,1024]{2,1,0:T(8,128)S(1)} %all_to_all.30, f32[2,1024,1024]{2,1,0:T(8,128)} %bitcast.45), kind=kOutput, calls=%fused_computation.7 | convolution fusion | flops 6447169536 | bytes 14680064 | tf_op jit(solution)/shard_map/btk,bko->tbo/dot_general | solution.py:30
  228.7 0.0 copy-start
  228.7 1.3 copy-done
  230.0 8.9 %fusion.22 = f32[2,1024,1024]{2,1,0:T(8,128)} fusion(f32[2,256,1024]{2,1,0:T(8,128)S(1)} %all_to_all.30, f32[256,2,1024]{2,0,1:T(8,128)S(1)} %fusion.6), kind=kOutput, calls=%fused_computation.20 | convolution fusion | flops 6442450944 | bytes 12582912 | tf_op jit(solution)/shard_map/btk,tbo->bko/dot_general | solution.py:34
  239.0 0.0 copy-start.1
  239.0 0.0 reduce-scatter.5.cloned.1.call-update
  239.0 0.3 reduce-scatter.3.cloned.1.call-start
  239.3 1.3 copy-done.1
  240.6 10.6 %fusion.21 = f32[2,256,1024]{2,1,0:T(8,128)} fusion(f32[256,2,1024]{2,0,1:T(8,128)S(1)} %copy-done.1, f32[2,1024,1024]{2,1,0:T(8,128)} %bitcast.46), kind=kOutput, calls=%fused_computation.19 | convolution fusion | flops 6442450944 | bytes 12582912 | tf_op jit(solution)/shard_map/tbo,bko->btk/dot_general | solution.py:35
  251.1 2.8 copy.51
  254.0 58.5 %all_to_all.38 = f32[2,256,1024]{1,0,2:T(2,128)S(1)} all-to-all(f32[2,256,1024]{1,0,2:T(2,128)S(1)} %copy.51), channel_id=1, replica_groups=mesh['blk'=8,'tok'=16] {'blk'}, dimensions={2} | all-to-all | bytes 4194304 | tf_op jit(solution)/shard_map/all_to_all | solution.py:36
  312.5 0.2 copy.52
  312.7 0.0 copy-start.3
  312.7 0.1 copy.53
  312.9 1.5 copy-done.3
  314.3 9.2 %fusion.10 = f32[2,16,64,1024]{3,2,1,0:T(8,128)} fusion(f32[16,256,2,64]{1,3,2,0:T(8,128)S(1)} %bitcast.56, f32[256,2,1024,1]{2,1,0,3:T(2,128)S(1)} %bitcast.51), kind=kOutput, calls=%fused_computation.12 | convolution fusion | flops 6442450944 | bytes 12582912 | tf_op jit(solution)/shard_map/tbi,stbg->bisg/dot_general | solution.py:38
  323.5 8.8 %copy.58 = f32[2,1024,1024]{2,1,0:T(8,128)} copy(f32[2,1024,1024]{1,2,0:T(8,128)} %bitcast.49) | data formatting | bytes 16777216 | tf_op jit(solution)/shard_map/reshape | solution.py:38
  332.3 0.0 reduce-scatter.3.cloned.1.call-update
  332.3 10.5 %fusion.18 = f32[256,2,1024]{2,0,1:T(8,128)} fusion(f32[16,256,2,64]{1,3,2,0:T(8,128)S(1)} %bitcast.57, f32[2,1024,16,64]{1,3,2,0:T(8,128)} %bitcast.48), kind=kOutput, calls=%fused_computation.18 | convolution fusion | flops 6442450944 | bytes 12582912 | tf_op jit(solution)/shard_map/stbg,bisg->tbi/dot_general | solution.py:41
  342.8 1.9 copy.55
  344.8 1.8 copy.60
  346.6 21.4 %reduce-scatter.5.cloned.1.call-done = f32[2,64,1024]{2,1,0:T(8,128)} async-done(((f32[2,1024,1024]{2,1,0:T(8,128)}), f32[2,64,1024]{2,1,0:T(8,128)}) %reduce-scatter.5.cloned.1.call-update) | async-done | bytes 524304 | tf_op jit(solution)/shard_map/reduce_scatter | solution.py:46
  368.0 101.4 %reduce-scatter.3.cloned.1.call-done = f32[2,64,1024]{2,1,0:T(8,128)} async-done(((f32[2,1024,1024]{2,1,0:T(8,128)}), f32[2,64,1024]{2,1,0:T(8,128)}) %reduce-scatter.3.cloned.1.call-update) | async-done | bytes 524304 | tf_op jit(solution)/shard_map/reduce_scatter | solution.py:45
Async XLA Ops:
  7.2 155.5 %all-gather.2.cloned.1.call-start = ((), (), s32[]{:S(2)}) async-start(), calls=%async_computation.5 | async-start | bytes 8912896 | tf_op jit(solution)/shard_map/all_gather | solution.py:22
  13.2 168.9 %all-to-all-start.1 = ((f32[16,2,64,1024]{3,2,1,0:T(8,128)}), f32[16,2,64,1024]{3,2,1,0:T(8,128)}, u32[]{:S(2)}, u32[]{:S(2)}) async-start(f32[16,2,64,1024]{3,2,1,0:T(8,128)} %stack.2), calls=%async_computation.1 | async-start | bytes 16777216 | tf_op jit(solution)/shard_map/all_to_all | solution.py:10
  22.4 149.0 %copy-start.2 = (f32[256,2,1024]{2,1,0:T(2,128)}, f32[256,2,1024]{2,1,0:T(2,128)S(1)}, u32[]{:S(2)}) copy-start(f32[256,2,1024]{2,1,0:T(2,128)S(1)} %reshape.38) | copy-start | bytes 6291460
  182.2 32.8 %all-to-all-start = ((f32[16,256,128]{1,2,0:T(8,128)}), f32[16,256,128]{1,2,0:T(8,128)S(1)}, u32[]{:S(2)}, u32[]{:S(2)}) async-start(f32[16,256,128]{1,2,0:T(8,128)} %bitcast.4), calls=%async_computation | async-start | bytes 4194304 | tf_op jit(solution)/shard_map/all_to_all | solution.py:29
  186.9 181.1 %reduce-scatter.5.cloned.1.call-start = ((), (), s32[]{:S(2)}) async-start(), calls=%async_computation.7 | async-start | bytes 8912896 | tf_op jit(solution)/shard_map/reduce_scatter | solution.py:46
  228.7 1.3 copy-start
  239.0 1.6 copy-start.1
  239.0 230.3 %reduce-scatter.3.cloned.1.call-start = ((), (), s32[]{:S(2)}) async-start(), calls=%async_computation.6 | async-start | bytes 8912896 | tf_op jit(solution)/shard_map/reduce_scatter | solution.py:45
  312.7 1.6 copy-start.3
Sparse Core Ops, SparseCore 0:
  9.7 152.9 all-gather.1
  239.1 128.8 reduce-scatter.4
  371.0 98.3 reduce-scatter.2
